TPU v7x, 32 devices: a whole 2x2x4 slice. The times are simulated.
32 devices in a mesh: groups: 2 (over y), seq: 16 (over z, x, core).
Axes of the slice: x: 2, y: 2, z: 4, core: 2. Of those that a mesh axis runs over, the one named last changes fastest.
Arguments:
- conv_input: bfloat16 [32768, 2304], P(('groups', 'seq')), parts along dimension 0, may hold values from -6 to 6
- gate_input: bfloat16 [32768, 2048], P(('groups', 'seq')), parts along dimension 0, may hold values from -6 to 6
- step_raw: bfloat16 [32768, 32], P(('groups', 'seq')), parts along dimension 0, may hold values from -1.5 to 1.5
- filter_taps: float32 [2, 4, 2304], replicated, may hold values from -3 to 3
- filter_bias: float32 [2, 2304], replicated, may hold values from -0.9 to -0.1
- step_bias: float32 [2, 32], replicated, may hold values from -4.5 to -3.5
- log_rate: float32 [2, 32], replicated
- skip_scale: float32 [2, 32], replicated, may hold values from 0.5 to 1.5
- norm_gain: float32 [2, 2048], replicated, may hold values from 0.5 to 1.5
Outputs:
- block_output: bfloat16 [32768, 2048], P(('groups', 'seq')), parts along dimension 0
There are 2 independent parts, one for each index of `groups`. A program takes and returns all parts, laid end to end along the dimension named above; an argument that names none is the same for every part. Nothing has to cross between parts.
All inputs are finite; a program needn't handle non-finite values.
Results may differ from a plain program's by a relative error of at most 0.018.
Values may be sent and summed in bfloat16 or wider, within the bound.
A program may use at most 192 MiB of HBM per device.

v0:
```python
import functools

import jax
import jax.numpy as jnp
from jax import lax
from jax.experimental import pallas as pl
from jax.experimental.pallas import tpu as pltpu
from jax.sharding import PartitionSpec as P

HEAD_DIM = 64
STATE = 128
CHUNK = 128
HALO = 16
LOG2E = 1.4426950408889634
F32 = jnp.float32
BF16 = jnp.bfloat16


def expander(heads, copies):
    row = lax.broadcasted_iota(jnp.int32, (heads * copies, heads * HEAD_DIM), 0) % heads
    col = lax.broadcasted_iota(jnp.int32, (heads * copies, heads * HEAD_DIM), 1) // HEAD_DIM
    return (row == col).astype(BF16)


def expand(values, matrix):
    high = values.astype(BF16)
    rest = values - high.astype(F32)
    low = rest.astype(BF16)
    parts = [high, low]
    heads = values.shape[1]
    if matrix.shape[0] == 3 * heads:
        parts.append((rest - low.astype(F32)).astype(BF16))
    return jnp.dot(jnp.concatenate(parts, axis=1), matrix, preferred_element_type=F32)


def prepare_kernel(
    heads,
    low_ref,
    high_ref,
    prev_ref,
    cur_ref,
    next_ref,
    raw_ref,
    taps_ref,
    bias_ref,
    sbias_ref,
    lrate_ref,
    e2_ref,
    e3_ref,
    u_ref,
    piece_ref,
    col_ref,
    row_ref,
    last_ref,
    dec_ref,
    buf,
    state,
    run,
):
    i = pl.program_id(0)
    count = pl.num_programs(0)
    inner = heads * HEAD_DIM
    channels = cur_ref.shape[1]

    @pl.when(i == 0)
    def _():
        buf[0:HALO] = low_ref[...].astype(F32)
        state[...] = jnp.zeros_like(state)
        run[...] = jnp.zeros_like(run)

    @pl.when(i > 0)
    def _():
        buf[0:HALO] = prev_ref[...].astype(F32)

    buf[HALO : HALO + CHUNK] = cur_ref[...].astype(F32)

    @pl.when(i == count - 1)
    def _():
        buf[HALO + CHUNK :] = high_ref[...].astype(F32)

    @pl.when(i < count - 1)
    def _():
        buf[HALO + CHUNK :] = next_ref[...].astype(F32)

    width = 256
    for c in range(channels // width):
        lanes = slice(c * width, (c + 1) * width)
        for k in range(2):
            half = None
            for j in range(4):
                start = HALO + (j - 3 if k == 0 else 3 - j)
                term = buf[start : start + CHUNK, lanes] * (0.5 * taps_ref[k, j : j + 1, lanes])
                half = 0.5 * bias_ref[k : k + 1, lanes] + term if half is None else half + term
            u_ref[k, :, lanes] = (half + half * jnp.tanh(half)).astype(BF16)

    t = lax.broadcasted_iota(jnp.int32, (CHUNK, CHUNK), 0)
    s = lax.broadcasted_iota(jnp.int32, (CHUNK, CHUNK), 1)
    raw = raw_ref[...].astype(F32)
    for k in range(2):
        dt = jax.nn.softplus(raw + sbias_ref[k : k + 1, :])
        a = dt * (-LOG2E * jnp.exp(lrate_ref[k : k + 1, :]))
        tri = ((s <= t) if k == 0 else (s >= t)).astype(F32)
        cum = jnp.dot(tri, a, precision=lax.Precision.HIGHEST, preferred_element_type=F32)
        end = cum[CHUNK - 1 : CHUNK] if k == 0 else cum[0:1]
        ahead = jnp.log2(dt) - cum
        col_ref[:, k * heads : (k + 1) * heads] = cum
        row_ref[k * heads : (k + 1) * heads, :] = ahead.T
        weight = expand(jnp.exp2(end + ahead), e2_ref[...])
        xs = (u_ref[k, :, :inner].astype(F32) * weight).astype(BF16)
        bt = u_ref[k, :, inner : inner + STATE].T
        piece = jnp.dot(bt, xs, preferred_element_type=F32)
        piece_ref[k, 0] = piece.astype(BF16)
        before = run[k : k + 1, :]
        if k == 0:
            factor = expand(jnp.broadcast_to(jnp.exp2(end), (8, heads)), e3_ref[...])[0:1]
            state[0] = state[0] * factor + piece
        else:
            factor = expand(jnp.broadcast_to(jnp.exp2(before), (8, heads)), e3_ref[...])[0:1]
            state[1] = state[1] + piece * factor
        run[k : k + 1, :] = before + end

    @pl.when(i == count - 1)
    def _():
        last_ref[...] = state[...].astype(BF16)
        dec_ref[...] = run[...]


def diagonal_kernel(heads, u_ref, col_ref, row_ref, skip_ref, y_ref):
    inner = heads * HEAD_DIM
    t = lax.broadcasted_iota(jnp.int32, (CHUNK, CHUNK), 0)
    s = lax.broadcasted_iota(jnp.int32, (CHUNK, CHUNK), 1)
    lane = lax.broadcasted_iota(jnp.int32, (CHUNK, CHUNK), 1)
    for k in range(2):
        b = u_ref[k, :, inner : inner + STATE]
        c = u_ref[k, :, inner + STATE :]
        scores = lax.dot_general(c, b, (((1,), (1,)), ((), ())), preferred_element_type=F32)
        scores = jnp.where((s <= t) if k == 0 else (s >= t), scores, 0.0)
        for pair in range(heads // 2):
            lanes = slice(pair * 128, (pair + 1) * 128)
            x = u_ref[k, :, lanes]
            weights = []
            for h in (2 * pair, 2 * pair + 1):
                n = k * heads + h
                gap = col_ref[:, n : n + 1] + row_ref[n : n + 1, :]
                weights.append((scores * jnp.exp2(jnp.minimum(gap, 64.0))).astype(BF16))
            zero = jnp.zeros_like(x)
            both = jnp.concatenate(
                [jnp.where(lane < HEAD_DIM, x, zero), jnp.where(lane >= HEAD_DIM, x, zero)], axis=0
            )
            y = jnp.dot(jnp.concatenate(weights, axis=1), both, preferred_element_type=F32)
            y_ref[k, :, lanes] = (y + x.astype(F32) * skip_ref[k : k + 1, lanes]).astype(BF16)


def finish_kernel(
    heads,
    y_ref,
    c_ref,
    col_ref,
    piece_ref,
    in_ref,
    gate_ref,
    gain_ref,
    e2_ref,
    e3_ref,
    out_ref,
    state,
    kept,
):
    step = pl.program_id(0)
    i = pl.program_id(1)
    count = pl.num_programs(1)

    @pl.when(i == 0)
    def _():
        state[...] = in_ref[0].astype(F32)

    def part(k):
        cum = col_ref[:, k * heads : (k + 1) * heads]
        end = cum[CHUNK - 1 : CHUNK] if k == 0 else cum[0:1]
        scale = expand(jnp.exp2(cum), e2_ref[...])
        carried = jnp.dot(c_ref[0], state[...].astype(BF16), preferred_element_type=F32)
        y = y_ref[0].astype(F32) + scale * carried
        half = 0.5 * gate_ref[...].astype(F32)
        g = y * (half + half * jnp.tanh(half))
        inverse = lax.rsqrt(jnp.mean(g * g, axis=-1, keepdims=True) + 1e-05)
        factor = expand(jnp.broadcast_to(jnp.exp2(end), (8, heads)), e3_ref[...])[0:1]
        state[...] = state[...] * factor + piece_ref[0, 0].astype(F32)
        return g * inverse * gain_ref[k : k + 1, :]

    @pl.when(step == 0)
    def _():
        at = pl.multiple_of((count - 1 - i) * CHUNK, CHUNK)
        kept[pl.ds(at, CHUNK), :] = part(1)

    @pl.when(step == 1)
    def _():
        at = pl.multiple_of(i * CHUNK, CHUNK)
        out_ref[...] = (kept[pl.ds(at, CHUNK), :] + part(0)).astype(BF16)


def passed_along(shard, by):
    devices = lax.axis_size("seq")
    pairs = [(i, i + by) for i in range(devices) if 0 <= i + by < devices]
    return lax.ppermute(shard, "seq", pairs)


def on_device(
    conv_input,
    gate_input,
    step_raw,
    filter_taps,
    filter_bias,
    step_bias,
    log_rate,
    skip_scale,
    norm_gain,
):
    length, channels = conv_input.shape
    heads = step_raw.shape[1]
    inner = heads * HEAD_DIM
    chunks = length // CHUNK
    low = passed_along(conv_input[length - HALO :], 1)
    high = passed_along(conv_input[:HALO], -1)
    e2 = expander(heads, 2)
    e3 = expander(heads, 3)
    per = CHUNK // HALO
    whole = lambda *shape: pl.BlockSpec(shape, lambda *_: (0,) * len(shape))
    params = pltpu.CompilerParams(vmem_limit_bytes=48 * 1024 * 1024)

    u, piece, col, row, last, dec = pl.pallas_call(
        functools.partial(prepare_kernel, heads),
        grid=(chunks,),
        in_specs=[
            whole(HALO, channels),
            whole(HALO, channels),
            pl.BlockSpec((HALO, channels), lambda i: (jnp.maximum(i * per - 1, 0), 0)),
            pl.BlockSpec((CHUNK, channels), lambda i: (i, 0)),
            pl.BlockSpec(
                (HALO, channels), lambda i: (jnp.minimum(i * per + per, chunks * per - 1), 0)
            ),
            pl.BlockSpec((CHUNK, heads), lambda i: (i, 0)),
            whole(*filter_taps.shape),
            whole(*filter_bias.shape),
            whole(2, heads),
            whole(2, heads),
            whole(*e2.shape),
            whole(*e3.shape),
        ],
        out_specs=[
            pl.BlockSpec((2, CHUNK, channels), lambda i: (0, i, 0)),
            pl.BlockSpec((2, 1, STATE, inner), lambda i: (0, i, 0, 0)),
            pl.BlockSpec((CHUNK, 2 * heads), lambda i: (i, 0)),
            pl.BlockSpec((2 * heads, CHUNK), lambda i: (0, i)),
            whole(2, STATE, inner),
            whole(2, heads),
        ],
        out_shape=[
            jax.ShapeDtypeStruct((2, length, channels), BF16),
            jax.ShapeDtypeStruct((2, chunks, STATE, inner), BF16),
            jax.ShapeDtypeStruct((length, 2 * heads), F32),
            jax.ShapeDtypeStruct((2 * heads, length), F32),
            jax.ShapeDtypeStruct((2, STATE, inner), BF16),
            jax.ShapeDtypeStruct((2, heads), F32),
        ],
        scratch_shapes=[
            pltpu.VMEM((CHUNK + 2 * HALO, channels), F32),
            pltpu.VMEM((2, STATE, inner), F32),
            pltpu.VMEM((2, heads), F32),
        ],
        compiler_params=params,
        cost_estimate=pl.CostEstimate(
            flops=2 * 2 * length * STATE * inner, bytes_accessed=25_000_000, transcendentals=0
        ),
    )(
        low,
        high,
        conv_input,
        conv_input,
        conv_input,
        step_raw,
        filter_taps,
        filter_bias,
        step_bias,
        log_rate,
        e2,
        e3,
    )

    def wide(logs):
        return jnp.repeat(jnp.exp2(logs), HEAD_DIM)[None, :]

    devices = lax.axis_size("seq")
    arriving = []
    for k in range(2):
        sign = 1 if k == 0 else -1
        total, held = passed_along((dec[k], last[k]), sign)
        held = held.astype(F32)
        offset = 1
        while offset < devices - 1:
            other, came = passed_along((total, held.astype(BF16)), sign * offset)
            held = held + wide(total) * came.astype(F32)
            total = total + other
            offset *= 2
        arriving.append(held.astype(BF16))

    local = pl.pallas_call(
        functools.partial(diagonal_kernel, heads),
        grid=(chunks,),
        in_specs=[
            pl.BlockSpec((2, CHUNK, channels), lambda i: (0, i, 0)),
            pl.BlockSpec((CHUNK, 2 * heads), lambda i: (i, 0)),
            pl.BlockSpec((2 * heads, CHUNK), lambda i: (0, i)),
            whole(2, inner),
        ],
        out_specs=pl.BlockSpec((2, CHUNK, inner), lambda i: (0, i, 0)),
        out_shape=jax.ShapeDtypeStruct((2, length, inner), BF16),
        compiler_params=params,
        cost_estimate=pl.CostEstimate(
            flops=20 * 2 * length * CHUNK * inner, bytes_accessed=20_000_000, transcendentals=0
        ),
    )(u, col, row, jnp.repeat(skip_scale, HEAD_DIM, axis=1))

    entering = jnp.stack(arriving)
    at = lambda p, i: jnp.where(p == 0, chunks - 1 - i, i)
    return pl.pallas_call(
        functools.partial(finish_kernel, heads),
        grid=(2, chunks),
        in_specs=[
            pl.BlockSpec((1, CHUNK, inner), lambda p, i: (1 - p, at(p, i), 0)),
            pl.BlockSpec((1, CHUNK, STATE), lambda p, i: (1 - p, at(p, i), inner // STATE + 1)),
            pl.BlockSpec((CHUNK, 2 * heads), lambda p, i: (at(p, i), 0)),
            pl.BlockSpec((1, 1, STATE, inner), lambda p, i: (1 - p, at(p, i), 0, 0)),
            pl.BlockSpec((1, STATE, inner), lambda p, i: (1 - p, 0, 0)),
            pl.BlockSpec((CHUNK, inner), lambda p, i: (at(p, i), 0)),
            whole(2, inner),
            whole(*e2.shape),
            whole(*e3.shape),
        ],
        out_specs=pl.BlockSpec((CHUNK, inner), lambda p, i: (jnp.where(p == 0, 0, i), 0)),
        out_shape=jax.ShapeDtypeStruct((length, inner), BF16),
        scratch_shapes=[
            pltpu.VMEM((STATE, inner), F32),
            pltpu.VMEM((length, inner), F32),
        ],
        compiler_params=params,
        cost_estimate=pl.CostEstimate(
            flops=2 * 2 * length * STATE * inner, bytes_accessed=30_000_000, transcendentals=0
        ),
    )(local, u, col, piece, entering, gate_input, norm_gain, e2, e3)


def solution(mesh):
    return jax.shard_map(
        on_device,
        mesh=mesh,
        in_specs=(P(("groups", "seq"), None),) * 3 + (P(),) * 6,
        out_specs=P(("groups", "seq"), None),
        check_vma=False,
    )
```

profile of v0, /device:TPU:0, one launch (start us, length us, event | category | flops | bytes accessed | tf_op | source)
XLA Modules:
  0.0 201.2 jit_solution(4621855586533721351)
XLA Ops:
  2.2 3.0 %collective-permute-start = (bf16[16,2304]{1,0:T(8,128)(2,1)S(1)}, bf16[16,2304]{1,0:T(8,128)(2,1)S(1)}, u32[]{:S(2)}, u32[]{:S(2)}) collective-permute-start(bf16[16,2304]{1,0:T(8,128)(2,1)S(1)} %get-tuple-element.26), channel_id=1, source_target_pairs={{0,1},{1,2},{2,3},{3,4},{4,5},{5,6},{6,7},{7,8},{8,9},{9,10},{10,1... | collective-permute-start | bytes 221192 | tf_op jit(solution)/shard_map/ppermute | solution.py:204
  10.5 29.3 %shard_map.91 = (bf16[2,1024,2304]{2,1,0:T(8,128)(2,1)}, bf16[2,8,128,2048]{3,2,1,0:T(8,128)(2,1)}, f32[1024,64]{1,0:T(8,128)S(1)}, f32[64,1024]{1,0:T(8,128)S(1...) custom-call(bf16[16,2304]{1,0:T(8,128)(2,1)S(1)} %collective-permute-done.low_ref, ...), custom_call_target="tpu_custom_call" | custom-call | flops 1073741824 | bytes 25000000 | tf_op jit(solution)/shard_map/pallas_call | solution.py:230
  39.8 4.4 %collective-permute-start.3 = (f32[32]{0:T(128)S(1)}, f32[32]{0:T(128)S(1)}, u32[]{:S(2)}, u32[]{:S(2)}) collective-permute-start(f32[32]{0:T(128)S(1)} %get-tuple-element.29), channel_id=1, source_target_pairs={{0,1},{1,2},{2,3},{3,4},{4,5},{5,6},{6,7},{7,8},{8,9},{9,10},{10,1... | collective-permute-start | bytes 392 | tf_op jit(solution)/shard_map/ppermute | solution.py:204
  45.6 4.1 %collective-permute-start.2 = (bf16[128,2048]{1,0:T(8,128)(2,1)S(1)}, bf16[128,2048]{1,0:T(8,128)(2,1)S(1)}, u32[]{:S(2)}, u32[]{:S(2)}) collective-permute-start(bf16[128,2048]{1,0:T(8,128)(2,1)S(1)} %get-tuple-element.27), channel_id=1, source_target_pairs={{0,1},{1,2},{2,3},{3,4},{4,5},{5,6},{6,7},{7,8},{8,9},{9,10},{10,1... | collective-permute-start | bytes 1572872 | tf_op jit(solution)/shard_map/ppermute | solution.py:204
  51.0 15.0 %shard_map.92.y_ref = bf16[2,1024,2048]{2,1,0:T(8,128)(2,1)} custom-call(bf16[2,1024,2304]{2,1,0:T(8,128)(2,1)} %get-tuple-element.11.u_ref.c_ref, f32[1024,64]{1,0:T(8,128)S(1)} %get-tuple-element.12.col_ref, f32[64,1024]{1,0:T(8,128)S(1)} %get-tuple-element.13.row_ref, f32[2,2048]{1,0:T(2,128)S(1)} %reshape.11.skip_ref), custom_call_target="tpu_custom_call" | custom-call | flops 10737418240 | bytes 20000000 | tf_op jit(solution)/shard_map/pallas_call | solution.py:306
  66.0 4.2 %collective-permute-start.5 = (f32[32]{0:T(128)S(1)}, f32[32]{0:T(128)S(1)}, u32[]{:S(2)}, u32[]{:S(2)}) collective-permute-start(f32[32]{0:T(128)S(1)} %collective-permute-done.3), channel_id=1, source_target_pairs={{0,1},{1,2},{2,3},{3,4},{4,5},{5,6},{6,7},{7,8},{8,9},{9,10},{10,1... | collective-permute-start | bytes 392 | tf_op jit(solution)/shard_map/ppermute | solution.py:204
  71.5 4.3 %collective-permute-start.4 = (bf16[128,2048]{1,0:T(8,128)(2,1)S(1)}, bf16[128,2048]{1,0:T(8,128)(2,1)S(1)}, u32[]{:S(2)}, u32[]{:S(2)}) collective-permute-start(bf16[128,2048]{1,0:T(8,128)(2,1)S(1)} %collective-permute-done.2), channel_id=1, source_target_pairs={{0,1},{1,2},{2,3},{3,4},{4,5},{5,6},{6,7},{7,8},{8,9},{9,10},{10,1... | collective-permute-start | bytes 1572872 | tf_op jit(solution)/shard_map/ppermute | solution.py:204
  75.9 6.9 %collective-permute-start.7 = (f32[32]{0:T(128)S(1)}, f32[32]{0:T(128)S(1)}, u32[]{:S(2)}, u32[]{:S(2)}) collective-permute-start(f32[32]{0:T(128)S(1)} %get-tuple-element.20), channel_id=1, source_target_pairs={{0,2},{1,3},{2,4},{3,5},{4,6},{5,7},{6,8},{7,9},{8,10},{9,11},{10,... | collective-permute-start | bytes 392 | tf_op jit(solution)/shard_map/ppermute | solution.py:204
  84.7 6.5 %collective-permute-start.9 = (f32[32]{0:T(128)S(1)}, f32[32]{0:T(128)S(1)}, u32[]{:S(2)}, u32[]{:S(2)}) collective-permute-start(f32[32]{0:T(128)S(1)} %get-tuple-element.18), channel_id=1, source_target_pairs={{0,4},{1,5},{2,6},{3,7},{4,8},{5,9},{6,10},{7,11},{8,12},{9,13},{1... | collective-permute-start | bytes 392 | tf_op jit(solution)/shard_map/ppermute | solution.py:204
  93.5 6.8 %collective-permute-start.6 = (bf16[128,2048]{1,0:T(8,128)(2,1)}, bf16[128,2048]{1,0:T(8,128)(2,1)}, u32[]{:S(2)}, u32[]{:S(2)}) collective-permute-start(bf16[128,2048]{1,0:T(8,128)(2,1)} %fusion), channel_id=1, source_target_pairs={{0,2},{1,3},{2,4},{3,5},{4,6},{5,7},{6,8},{7,9},{8,10},{9,11},{10,... | collective-permute-start | bytes 1572872 | tf_op jit(solution)/shard_map/ppermute | solution.py:204
  104.5 14.5 %collective-permute-done.6 = bf16[128,2048]{1,0:T(8,128)(2,1)} collective-permute-done((bf16[128,2048]{1,0:T(8,128)(2,1)}, bf16[128,2048]{1,0:T(8,128)(2,1)}, u32[]{:S(2)}, u32[]{:S(2)}) %collective-permute-start.6) | collective-permute-done | bytes 524320 | tf_op jit(solution)/shard_map/ppermute | solution.py:204
  120.3 1.3 collective-permute-start.8
  121.6 2.1 %fusion.9 = bf16[128,2048]{1,0:T(8,128)(2,1)} fusion(bf16[128,2048]{1,0:T(8,128)(2,1)S(1)} %collective-permute-done.15, f32[2048]{0:T(1024)S(1)} %mul.95, bf16[128,2048]{1,0:T(8,128)(2,1)} %collective-permute-done.13, f32[2048]{0:T(1024)S(1)} %mul.92, bf16[128,2048]{1,0:T(8,128)(2,1)S(1)} %collective-permute-done.11), kind=kLoop, calls=%fused_computation.25 | loop fusion | flops 2097152 | bytes 2113536 | tf_op jit(solution)/shard_map/convert_element_type | solution.py:300
  125.0 8.5 %collective-permute-done.8 = bf16[128,2048]{1,0:T(8,128)(2,1)S(1)} collective-permute-done((bf16[128,2048]{1,0:T(8,128)(2,1)S(1)}, bf16[128,2048]{1,0:T(8,128)(2,1)S(1)}, u32[]{:S(2)}, u32[]{:S(2)}) %collective-permute-start.8) | collective-permute-done | bytes 524320 | tf_op jit(solution)/shard_map/ppermute | solution.py:204
  134.3 2.2 %fusion.3 = bf16[128,2048]{1,0:T(8,128)(2,1)} fusion(bf16[128,2048]{1,0:T(8,128)(2,1)S(1)} %collective-permute-done.8, f32[2048]{0:T(1024)S(1)} %mul.86, bf16[128,2048]{1,0:T(8,128)(2,1)} %collective-permute-done.6, f32[2048]{0:T(1024)S(1)} %mul.83, bf16[128,2048]{1,0:T(8,128)(2,1)S(1)} %collective-permute-done.4, f32[2048]{0:T(1024)S(1)} %mul.80, ...), kind=kLoop, calls=%fused_computation.13 | loop fusion | flops 2883584 | bytes 2646016 | tf_op jit(solution)/shard_map/convert_element_type | solution.py:300
  136.5 7.0 %collective-permute-start.10 = (bf16[128,2048]{1,0:T(8,128)(2,1)}, bf16[128,2048]{1,0:T(8,128)(2,1)}, u32[]{:S(2)}, u32[]{:S(2)}) collective-permute-start(bf16[128,2048]{1,0:T(8,128)(2,1)} %fusion.3), channel_id=1, source_target_pairs={{0,8},{1,9},{2,10},{3,11},{4,12},{5,13},{6,14},{7,15},{16,24},{17,... | collective-permute-start | bytes 1572872 | tf_op jit(solution)/shard_map/ppermute | solution.py:204
  143.8 3.0 %collective-permute-done.17 = bf16[128,2048]{1,0:T(8,128)(2,1)} collective-permute-done((bf16[128,2048]{1,0:T(8,128)(2,1)}, bf16[128,2048]{1,0:T(8,128)(2,1)}, u32[]{:S(2)}, u32[]{:S(2)}) %collective-permute-start.17) | collective-permute-done | bytes 524320 | tf_op jit(solution)/shard_map/ppermute | solution.py:204
  146.8 1.6 fusion.4
  148.4 1.5 collective-permute-start.19
  149.9 4.2 %collective-permute-done.10 = bf16[128,2048]{1,0:T(8,128)(2,1)} collective-permute-done((bf16[128,2048]{1,0:T(8,128)(2,1)}, bf16[128,2048]{1,0:T(8,128)(2,1)}, u32[]{:S(2)}, u32[]{:S(2)}) %collective-permute-start.10) | collective-permute-done | bytes 524320 | tf_op jit(solution)/shard_map/ppermute | solution.py:204
  154.1 1.8 fusion.5
  156.0 21.6 %collective-permute-done.19 = bf16[128,2048]{1,0:T(8,128)(2,1)S(1)} collective-permute-done((bf16[128,2048]{1,0:T(8,128)(2,1)S(1)}, bf16[128,2048]{1,0:T(8,128)(2,1)S(1)}, u32[]{:S(2)}, u32[]{:S(2)}) %collective-permute-start.19) | collective-permute-done | bytes 524320 | tf_op jit(solution)/shard_map/ppermute | solution.py:204
  177.6 1.7 fusion.6
  179.4 21.8 %shard_map.93 = bf16[1024,2048]{1,0:T(8,128)(2,1)} custom-call(bf16[2,1024,2048]{2,1,0:T(8,128)(2,1)} %shard_map.92.y_ref, bf16[2,1024,2304]{2,1,0:T(8,128)(2,1)} %get-tuple-element.11.u_ref.c_ref, f32[1024,64]{1,0:T(8,128)S(1)} %get-tuple-element.12.col_ref, bf16[2,8,128,2048]{3,2,1,0:T(8,128)(2,1)} %get-tuple-element.14.piece_ref, ...), custom_call_target="tpu_custom_call" | custom-call | flops 1073741824 | bytes 30000000 | tf_op jit(solution)/shard_map/pallas_call | solution.py:325
  (76 shorter events, 23.4 us)
Async XLA Ops:
  0.9 6.6 %collective-permute-start.1 = (bf16[16,2304]{1,0:T(8,128)(2,1)S(1)}, bf16[16,2304]{1,0:T(8,128)(2,1)S(1)}, u32[]{:S(2)}, u32[]{:S(2)}) collective-permute-start(bf16[16,2304]{1,0:T(8,128)(2,1)S(1)} %get-tuple-element.25), channel_id=1, source_target_pairs={{1,0},{2,1},{3,2},{4,3},{5,4},{6,5},{7,6},{8,7},{9,8},{10,9},{11,1... | collective-permute-start | bytes 221192 | tf_op jit(solution)/shard_map/ppermute | solution.py:204
  2.2 5.3 %collective-permute-start = (bf16[16,2304]{1,0:T(8,128)(2,1)S(1)}, bf16[16,2304]{1,0:T(8,128)(2,1)S(1)}, u32[]{:S(2)}, u32[]{:S(2)}) collective-permute-start(bf16[16,2304]{1,0:T(8,128)(2,1)S(1)} %get-tuple-element.26), channel_id=1, source_target_pairs={{0,1},{1,2},{2,3},{3,4},{4,5},{5,6},{6,7},{7,8},{8,9},{9,10},{10,1... | collective-permute-start | bytes 221192 | tf_op jit(solution)/shard_map/ppermute | solution.py:204
  7.5 0.9 copy-start
  8.4 0.7 copy-start.1
  39.8 26.2 %collective-permute-start.3 = (f32[32]{0:T(128)S(1)}, f32[32]{0:T(128)S(1)}, u32[]{:S(2)}, u32[]{:S(2)}) collective-permute-start(f32[32]{0:T(128)S(1)} %get-tuple-element.29), channel_id=1, source_target_pairs={{0,1},{1,2},{2,3},{3,4},{4,5},{5,6},{6,7},{7,8},{8,9},{9,10},{10,1... | collective-permute-start | bytes 392 | tf_op jit(solution)/shard_map/ppermute | solution.py:204
  44.2 26.0 %collective-permute-start.12 = (f32[32]{0:T(128)S(1)}, f32[32]{0:T(128)S(1)}, u32[]{:S(2)}, u32[]{:S(2)}) collective-permute-start(f32[32]{0:T(128)S(1)} %get-tuple-element.30), channel_id=1, source_target_pairs={{1,0},{2,1},{3,2},{4,3},{5,4},{6,5},{7,6},{8,7},{9,8},{10,9},{11,1... | collective-permute-start | bytes 392 | tf_op jit(solution)/shard_map/ppermute | solution.py:204
  45.6 25.9 %collective-permute-start.2 = (bf16[128,2048]{1,0:T(8,128)(2,1)S(1)}, bf16[128,2048]{1,0:T(8,128)(2,1)S(1)}, u32[]{:S(2)}, u32[]{:S(2)}) collective-permute-start(bf16[128,2048]{1,0:T(8,128)(2,1)S(1)} %get-tuple-element.27), channel_id=1, source_target_pairs={{0,1},{1,2},{2,3},{3,4},{4,5},{5,6},{6,7},{7,8},{8,9},{9,10},{10,1... | collective-permute-start | bytes 1572872 | tf_op jit(solution)/shard_map/ppermute | solution.py:204
  49.7 41.6 %collective-permute-start.11 = (bf16[128,2048]{1,0:T(8,128)(2,1)S(1)}, bf16[128,2048]{1,0:T(8,128)(2,1)S(1)}, u32[]{:S(2)}, u32[]{:S(2)}) collective-permute-start(bf16[128,2048]{1,0:T(8,128)(2,1)S(1)} %get-tuple-element.28), channel_id=1, source_target_pairs={{1,0},{2,1},{3,2},{4,3},{5,4},{6,5},{7,6},{8,7},{9,8},{10,9},{11,1... | collective-permute-start | bytes 1572872 | tf_op jit(solution)/shard_map/ppermute | solution.py:204
  66.0 9.9 %collective-permute-start.5 = (f32[32]{0:T(128)S(1)}, f32[32]{0:T(128)S(1)}, u32[]{:S(2)}, u32[]{:S(2)}) collective-permute-start(f32[32]{0:T(128)S(1)} %collective-permute-done.3), channel_id=1, source_target_pairs={{0,1},{1,2},{2,3},{3,4},{4,5},{5,6},{6,7},{7,8},{8,9},{9,10},{10,1... | collective-permute-start | bytes 392 | tf_op jit(solution)/shard_map/ppermute | solution.py:204
  70.2 12.6 %collective-permute-start.14 = (f32[32]{0:T(128)S(1)}, f32[32]{0:T(128)S(1)}, u32[]{:S(2)}, u32[]{:S(2)}) collective-permute-start(f32[32]{0:T(128)S(1)} %collective-permute-done.12), channel_id=1, source_target_pairs={{1,0},{2,1},{3,2},{4,3},{5,4},{6,5},{7,6},{8,7},{9,8},{10,9},{11,1... | collective-permute-start | bytes 392 | tf_op jit(solution)/shard_map/ppermute | solution.py:204
  71.5 21.0 %collective-permute-start.4 = (bf16[128,2048]{1,0:T(8,128)(2,1)S(1)}, bf16[128,2048]{1,0:T(8,128)(2,1)S(1)}, u32[]{:S(2)}, u32[]{:S(2)}) collective-permute-start(bf16[128,2048]{1,0:T(8,128)(2,1)S(1)} %collective-permute-done.2), channel_id=1, source_target_pairs={{0,1},{1,2},{2,3},{3,4},{4,5},{5,6},{6,7},{7,8},{8,9},{9,10},{10,1... | collective-permute-start | bytes 1572872 | tf_op jit(solution)/shard_map/ppermute | solution.py:204
  75.9 8.8 %collective-permute-start.7 = (f32[32]{0:T(128)S(1)}, f32[32]{0:T(128)S(1)}, u32[]{:S(2)}, u32[]{:S(2)}) collective-permute-start(f32[32]{0:T(128)S(1)} %get-tuple-element.20), channel_id=1, source_target_pairs={{0,2},{1,3},{2,4},{3,5},{4,6},{5,7},{6,8},{7,9},{8,10},{9,11},{10,... | collective-permute-start | bytes 392 | tf_op jit(solution)/shard_map/ppermute | solution.py:204
  82.8 17.5 %collective-permute-start.16 = (f32[32]{0:T(128)S(1)}, f32[32]{0:T(128)S(1)}, u32[]{:S(2)}, u32[]{:S(2)}) collective-permute-start(f32[32]{0:T(128)S(1)} %get-tuple-element.24), channel_id=1, source_target_pairs={{2,0},{3,1},{4,2},{5,3},{6,4},{7,5},{8,6},{9,7},{10,8},{11,9},{12,... | collective-permute-start | bytes 392 | tf_op jit(solution)/shard_map/ppermute | solution.py:204
  84.7 36.8 %collective-permute-start.9 = (f32[32]{0:T(128)S(1)}, f32[32]{0:T(128)S(1)}, u32[]{:S(2)}, u32[]{:S(2)}) collective-permute-start(f32[32]{0:T(128)S(1)} %get-tuple-element.18), channel_id=1, source_target_pairs={{0,4},{1,5},{2,6},{3,7},{4,8},{5,9},{6,10},{7,11},{8,12},{9,13},{1... | collective-permute-start | bytes 392 | tf_op jit(solution)/shard_map/ppermute | solution.py:204
  91.3 10.7 %collective-permute-start.13 = (bf16[128,2048]{1,0:T(8,128)(2,1)S(1)}, bf16[128,2048]{1,0:T(8,128)(2,1)}, u32[]{:S(2)}, u32[]{:S(2)}) collective-permute-start(bf16[128,2048]{1,0:T(8,128)(2,1)S(1)} %collective-permute-done.11), channel_id=1, source_target_pairs={{1,0},{2,1},{3,2},{4,3},{5,4},{6,5},{7,6},{8,7},{9,8},{10,9},{11,1... | collective-permute-start | bytes 1572872 | tf_op jit(solution)/shard_map/ppermute | solution.py:204
  93.5 25.4 %collective-permute-start.6 = (bf16[128,2048]{1,0:T(8,128)(2,1)}, bf16[128,2048]{1,0:T(8,128)(2,1)}, u32[]{:S(2)}, u32[]{:S(2)}) collective-permute-start(bf16[128,2048]{1,0:T(8,128)(2,1)} %fusion), channel_id=1, source_target_pairs={{0,2},{1,3},{2,4},{3,5},{4,6},{5,7},{6,8},{7,9},{8,10},{9,11},{10,... | collective-permute-start | bytes 1572872 | tf_op jit(solution)/shard_map/ppermute | solution.py:204
  100.4 43.1 %collective-permute-start.18 = (f32[32]{0:T(128)S(1)}, f32[32]{0:T(128)S(1)}, u32[]{:S(2)}, u32[]{:S(2)}) collective-permute-start(f32[32]{0:T(128)S(1)} %get-tuple-element.22), channel_id=1, source_target_pairs={{4,0},{5,1},{6,2},{7,3},{8,4},{9,5},{10,6},{11,7},{12,8},{13,9},{1... | collective-permute-start | bytes 392 | tf_op jit(solution)/shard_map/ppermute | solution.py:204
  103.2 18.4 %collective-permute-start.15 = (bf16[128,2048]{1,0:T(8,128)(2,1)S(1)}, bf16[128,2048]{1,0:T(8,128)(2,1)S(1)}, u32[]{:S(2)}, u32[]{:S(2)}) collective-permute-start(bf16[128,2048]{1,0:T(8,128)(2,1)S(1)} %fusion.1), channel_id=1, source_target_pairs={{2,0},{3,1},{4,2},{5,3},{6,4},{7,5},{8,6},{9,7},{10,8},{11,9},{12,... | collective-permute-start | bytes 1572872 | tf_op jit(solution)/shard_map/ppermute | solution.py:204
  120.3 13.2 %collective-permute-start.8 = (bf16[128,2048]{1,0:T(8,128)(2,1)S(1)}, bf16[128,2048]{1,0:T(8,128)(2,1)S(1)}, u32[]{:S(2)}, u32[]{:S(2)}) collective-permute-start(bf16[128,2048]{1,0:T(8,128)(2,1)S(1)} %fusion.8), channel_id=1, source_target_pairs={{0,4},{1,5},{2,6},{3,7},{4,8},{5,9},{6,10},{7,11},{8,12},{9,13},{1... | collective-permute-start | bytes 1572872 | tf_op jit(solution)/shard_map/ppermute | solution.py:204
  123.7 23.1 %collective-permute-start.17 = (bf16[128,2048]{1,0:T(8,128)(2,1)}, bf16[128,2048]{1,0:T(8,128)(2,1)}, u32[]{:S(2)}, u32[]{:S(2)}) collective-permute-start(bf16[128,2048]{1,0:T(8,128)(2,1)} %fusion.9), channel_id=1, source_target_pairs={{4,0},{5,1},{6,2},{7,3},{8,4},{9,5},{10,6},{11,7},{12,8},{13,9},{1... | collective-permute-start | bytes 1572872 | tf_op jit(solution)/shard_map/ppermute | solution.py:204
  133.5 0.8 copy-start.5
  136.5 17.6 %collective-permute-start.10 = (bf16[128,2048]{1,0:T(8,128)(2,1)}, bf16[128,2048]{1,0:T(8,128)(2,1)}, u32[]{:S(2)}, u32[]{:S(2)}) collective-permute-start(bf16[128,2048]{1,0:T(8,128)(2,1)} %fusion.3), channel_id=1, source_target_pairs={{0,8},{1,9},{2,10},{3,11},{4,12},{5,13},{6,14},{7,15},{16,24},{17,... | collective-permute-start | bytes 1572872 | tf_op jit(solution)/shard_map/ppermute | solution.py:204
  148.4 31.0 %copy-start.2 = (f32[2,2048]{1,0:T(2,128)S(1)}, f32[2,2048]{1,0:T(2,128)}, u32[]{:S(2)}) copy-start(f32[2,2048]{1,0:T(2,128)} %gain_ref.1) | copy-start | bytes 49156
  148.4 29.2 %collective-permute-start.19 = (bf16[128,2048]{1,0:T(8,128)(2,1)S(1)}, bf16[128,2048]{1,0:T(8,128)(2,1)S(1)}, u32[]{:S(2)}, u32[]{:S(2)}) collective-permute-start(bf16[128,2048]{1,0:T(8,128)(2,1)S(1)} %fusion.4), channel_id=1, source_target_pairs={{8,0},{9,1},{10,2},{11,3},{12,4},{13,5},{14,6},{15,7},{24,16},{25,... | collective-permute-start | bytes 1572872 | tf_op jit(solution)/shard_map/ppermute | solution.py:204
  (2 other events, 1.4 us)
where the time goes:
time: 203 us; the launch traced here: 201 us
  Pallas kernels  66.1 us (33%)
  starting transfers between devices  61.7 us (30%)
  waiting for transfers between devices  51.8 us (26%)
  other arithmetic  13.4 us (7%)
  local copies, waits for them, and re-layouts  7.76 us (4%)
    ppermute x20, starting transfers between devices, passed_along(): return lax.ppermute(shard, 'seq', pairs)  61.7 us
    ppermute x20, waiting for transfers between devices, passed_along(): return lax.ppermute(shard, 'seq', pairs)  51.8 us
    pallas_call x1, Pallas kernels, on_device(): pl.pallas_call(functools.partial(prepare_kernel, heads), grid=(chunks,),...  29.3 us
    pallas_call x1, Pallas kernels, on_device(): pl.pallas_call(functools.partial(finish_kernel, heads), grid=(2, chunks),...  21.8 us
    pallas_call x1, Pallas kernels, on_device(): pl.pallas_call(functools.partial(diagonal_kernel, heads), grid=(chunks,),...  15 us
    convert_element_type x6, other arithmetic, on_device(): other, came = passed_along((total, held.astype(BF16)), sign * offset)  9.42 us
    unnamed x13, local copies, waits for them, and re-layouts  4.76 us
  transfers between devices with their start and end apart: 20, of which 5 were waited for; matrix products, arithmetic and copies ran while one was open for 7% of the time, Pallas kernels for 7%

commit v1 on v0

v1 whole, which is shorter than its diff:
```python
import functools

import jax
import jax.numpy as jnp
from jax import lax
from jax.experimental import pallas as pl
from jax.experimental.pallas import tpu as pltpu
from jax.sharding import PartitionSpec as P

HEAD_DIM = 64
STATE = 128
CHUNK = 128
HALO = 16
TILE = 16
MESH = pl.DeviceIdType.MESH
LOG2E = 1.4426950408889634
F32 = jnp.float32
BF16 = jnp.bfloat16


def expander(heads, copies):
    row = lax.broadcasted_iota(jnp.int32, (heads * copies, heads * HEAD_DIM), 0) % heads
    col = lax.broadcasted_iota(jnp.int32, (heads * copies, heads * HEAD_DIM), 1) // HEAD_DIM
    return (row == col).astype(BF16)


def expand(values, matrix):
    high = values.astype(BF16)
    rest = values - high.astype(F32)
    low = rest.astype(BF16)
    parts = [high, low]
    heads = values.shape[1]
    if matrix.shape[0] == 3 * heads:
        parts.append((rest - low.astype(F32)).astype(BF16))
    return jnp.dot(jnp.concatenate(parts, axis=1), matrix, preferred_element_type=F32)


def mixer_kernel(
    heads,
    n,
    tail_ref,
    head_ref,
    prev_ref,
    cur_ref,
    next_ref,
    raw_ref,
    gate_ref,
    taps_ref,
    bias_ref,
    sbias_ref,
    lrate_ref,
    skip_ref,
    gain_ref,
    e2_ref,
    e3_ref,
    out_ref,
    buf,
    u,
    piece,
    local,
    kept,
    cols,
    rows,
    state,
    run,
    edge,
    halo,
    message,
    got,
    reply,
    entering,
    edge_send,
    edge_recv,
    send_sem,
    recv_sem,
):
    step = pl.program_id(0)
    chunks = u.shape[1]
    inner = heads * HEAD_DIM
    channels = cur_ref.shape[1]
    me = lax.axis_index("seq")
    height = STATE * (inner // 128) // n
    share = lambda o: (
        slice(o * height % STATE, o * height % STATE + height),
        slice(o * height // STATE * 128, o * height // STATE * 128 + 128),
    )

    def to_edge(side):
        return pltpu.make_async_remote_copy(
            src_ref=edge.at[side],
            dst_ref=halo.at[side],
            send_sem=edge_send.at[side],
            recv_sem=edge_recv.at[side],
            device_id={"seq": lax.rem(me + (1 if side == 0 else n - 1), n)},
            device_id_type=MESH,
        )

    def to_all(source, target, number, k):
        @pl.loop(1, n)
        def _(p):
            peer = lax.rem(me + p, n)
            pltpu.make_async_remote_copy(
                src_ref=source.at[k, peer],
                dst_ref=target.at[k, me],
                send_sem=send_sem.at[number],
                recv_sem=recv_sem.at[number],
                device_id={"seq": peer},
                device_id_type=MESH,
            ).start()

    def wait_all(ref, sem, k):
        part = ref.at[k, pl.ds(0, n - 1)]
        pltpu.make_async_copy(part, part, sem).wait()

    @pl.when(step == 0)
    def _():
        barrier = pltpu.get_barrier_semaphore()

        @pl.loop(1, n)
        def _(p):
            pl.semaphore_signal(
                barrier, inc=1, device_id={"seq": lax.rem(me + p, n)}, device_id_type=MESH
            )

        edge[0] = tail_ref[...]
        edge[1] = head_ref[...]
        pl.semaphore_wait(barrier, n - 1)
        to_edge(0).start()
        to_edge(1).start()

    t = lax.broadcasted_iota(jnp.int32, (CHUNK, CHUNK), 0)
    s = lax.broadcasted_iota(jnp.int32, (CHUNK, CHUNK), 1)

    def prepare(k, at, first, last):
        @pl.when(first)
        def _():
            state[...] = jnp.zeros_like(state)
            run[...] = jnp.zeros_like(run)

        buf[0:HALO] = prev_ref[...].astype(F32)
        buf[HALO : HALO + CHUNK] = cur_ref[...].astype(F32)
        buf[HALO + CHUNK :] = next_ref[...].astype(F32)

        @pl.when(last)
        def _():
            to_edge(k).wait()
            if k == 0:
                buf[0:HALO] = jnp.where(me == 0, 0.0, halo[0].astype(F32))
            else:
                buf[HALO + CHUNK :] = jnp.where(me == n - 1, 0.0, halo[1].astype(F32))

        width = 256
        for c in range(channels // width):
            lanes = slice(c * width, (c + 1) * width)
            half = None
            for j in range(4):
                start = HALO + (j - 3 if k == 0 else 3 - j)
                term = buf[start : start + CHUNK, lanes] * (0.5 * taps_ref[k, j : j + 1, lanes])
                half = 0.5 * bias_ref[k : k + 1, lanes] + term if half is None else half + term
            u[k, at, :, lanes] = (half + half * jnp.tanh(half)).astype(BF16)

        dt = jax.nn.softplus(raw_ref[...].astype(F32) + sbias_ref[k : k + 1, :])
        a = dt * (-LOG2E * jnp.exp(lrate_ref[k : k + 1, :]))
        tri = ((s <= t) if k == 0 else (s >= t)).astype(F32)
        cum = jnp.dot(tri, a, precision=lax.Precision.HIGHEST, preferred_element_type=F32)
        end = cum[CHUNK - 1 : CHUNK] if k == 0 else cum[0:1]
        ahead = jnp.log2(dt) - cum
        cols[k, at] = cum
        rows[k, at] = ahead.T
        weight = expand(jnp.exp2(end + ahead), e2_ref[...])
        xs = (u[k, at, :, :inner].astype(F32) * weight).astype(BF16)
        bt = u[k, at, :, inner : inner + STATE].T
        part = jnp.dot(bt, xs, preferred_element_type=F32)
        piece[k, at] = part.astype(BF16)
        before = run[0:1, :]
        factor = expand(jnp.broadcast_to(jnp.exp2(before), (8, heads)), e3_ref[...])[0:1]
        state[...] = state[...] + part * factor
        run[0:1, :] = before + end

        @pl.when(last)
        def _():
            decay = expand(jnp.exp2(jnp.broadcast_to(run[0:1, :], (TILE, heads))), e3_ref[...])
            high = decay.astype(BF16).astype(F32)
            which = lax.broadcasted_iota(jnp.int32, (TILE, inner), 0)
            tile = jnp.where(which == 0, high, jnp.where(which == 1, decay - high, 0.0))
            for o in range(n):
                where = share(o)
                message[k, o, 0:height] = state[where].astype(BF16)
                message[k, o, height:] = tile[:, where[1]].astype(BF16)
            got[k, me] = message[k, me]
            to_all(message, got, k, k)

    def scan(k):
        wait_all(got, recv_sem.at[k], k)

        def one(j, held):
            j = j if k == 0 else n - 1 - j
            reply[k, j] = held.astype(BF16)
            tile = got[k, j, height:].astype(F32)
            return held * (tile[0:1] + tile[1:2]) + got[k, j, 0:height].astype(F32)

        lax.fori_loop(0, n, one, jnp.zeros((height, 128), F32))
        entering[k, me] = reply[k, me]
        to_all(reply, entering, 2 + k, k)

    def diagonal(k, at):
        b = u[k, at, :, inner : inner + STATE]
        c = u[k, at, :, inner + STATE :]
        scores = lax.dot_general(c, b, (((1,), (1,)), ((), ())), preferred_element_type=F32)
        scores = jnp.where((s <= t) if k == 0 else (s >= t), scores, 0.0)
        for pair in range(heads // 2):
            lanes = slice(pair * 128, (pair + 1) * 128)
            x = u[k, at, :, lanes]
            weights = []
            for h in (2 * pair, 2 * pair + 1):
                gap = cols[k, at, :, h : h + 1] + rows[k, at, h : h + 1, :]
                weights.append((scores * jnp.exp2(jnp.minimum(gap, 64.0))).astype(BF16))
            zero = jnp.zeros_like(x)
            both = jnp.concatenate(
                [jnp.where(s < HEAD_DIM, x, zero), jnp.where(s >= HEAD_DIM, x, zero)], axis=0
            )
            y = jnp.dot(jnp.concatenate(weights, axis=1), both, preferred_element_type=F32)
            local[k, at, :, lanes] = (y + x.astype(F32) * skip_ref[k : k + 1, lanes]).astype(BF16)

    def finish(k, at, first):
        @pl.when(first)
        def _():
            wait_all(entering, recv_sem.at[2 + k], k)
            for o in range(n):
                state[share(o)] = entering[k, o].astype(F32)

        cum = cols[k, at]
        end = cum[CHUNK - 1 : CHUNK] if k == 0 else cum[0:1]
        scale = expand(jnp.exp2(cum), e2_ref[...])
        carried = jnp.dot(
            u[k, at, :, inner + STATE :], state[...].astype(BF16), preferred_element_type=F32
        )
        y = local[k, at].astype(F32) + scale * carried
        half = 0.5 * gate_ref[...].astype(F32)
        g = y * (half + half * jnp.tanh(half))
        inverse = lax.rsqrt(jnp.mean(g * g, axis=-1, keepdims=True) + 1e-05)
        factor = expand(jnp.broadcast_to(jnp.exp2(end), (8, heads)), e3_ref[...])[0:1]
        state[...] = state[...] * factor + piece[k, at].astype(F32)
        return g * inverse * gain_ref[k : k + 1, :]

    @pl.when(step < chunks)
    def _():
        prepare(0, chunks - 1 - step, step == 0, step == chunks - 1)

    @pl.when((step >= chunks) & (step < 2 * chunks))
    def _():
        prepare(1, step - chunks, step == chunks, step == 2 * chunks - 1)

    @pl.when(step == 2 * chunks)
    def _():
        scan(0)

    @pl.when(step == 3 * chunks - 2)
    def _():
        scan(1)

    @pl.when((step >= 2 * chunks) & (step < 3 * chunks))
    def _():
        at = step - 2 * chunks
        diagonal(0, at)
        diagonal(1, at)

    @pl.when((step >= 3 * chunks) & (step < 4 * chunks))
    def _():
        at = step - 3 * chunks
        kept[at] = finish(0, at, step == 3 * chunks)

    @pl.when(step >= 4 * chunks)
    def _():
        at = 5 * chunks - 1 - step
        out_ref[...] = (kept[at] + finish(1, at, step == 4 * chunks)).astype(BF16)

    @pl.when(step == 5 * chunks - 1)
    def _():
        for k in range(2):
            wait_all(message, send_sem.at[k], k)
            wait_all(reply, send_sem.at[2 + k], k)


def on_device(
    conv_input,
    gate_input,
    step_raw,
    filter_taps,
    filter_bias,
    step_bias,
    log_rate,
    skip_scale,
    norm_gain,
):
    length, channels = conv_input.shape
    heads = step_raw.shape[1]
    inner = heads * HEAD_DIM
    chunks = length // CHUNK
    n = lax.axis_size("seq")
    height = STATE * (inner // 128) // n
    e2 = expander(heads, 2)
    e3 = expander(heads, 3)
    per = CHUNK // HALO
    last = chunks * per - 1
    whole = lambda *shape: pl.BlockSpec(shape, lambda *_: (0,) * len(shape))

    def taken(i):
        return jnp.where(i < chunks, chunks - 1 - i, jnp.minimum(i - chunks, chunks - 1))

    def given(i):
        return jnp.where(i < 4 * chunks, jnp.clip(i - 3 * chunks, 0, chunks - 1), 5 * chunks - 1 - i)

    return pl.pallas_call(
        functools.partial(mixer_kernel, heads, n),
        grid=(5 * chunks,),
        in_specs=[
            pl.BlockSpec((HALO, channels), lambda i: (last, 0)),
            pl.BlockSpec((HALO, channels), lambda i: (0, 0)),
            pl.BlockSpec((HALO, channels), lambda i: (jnp.maximum(taken(i) * per - 1, 0), 0)),
            pl.BlockSpec((CHUNK, channels), lambda i: (taken(i), 0)),
            pl.BlockSpec((HALO, channels), lambda i: (jnp.minimum(taken(i) * per + per, last), 0)),
            pl.BlockSpec((CHUNK, heads), lambda i: (taken(i), 0)),
            pl.BlockSpec((CHUNK, inner), lambda i: (given(i), 0)),
            whole(*filter_taps.shape),
            whole(*filter_bias.shape),
            whole(2, heads),
            whole(2, heads),
            whole(2, inner),
            whole(2, inner),
            whole(*e2.shape),
            whole(*e3.shape),
        ],
        out_specs=pl.BlockSpec(
            (CHUNK, inner), lambda i: (jnp.minimum(5 * chunks - 1 - i, chunks - 1), 0)
        ),
        out_shape=jax.ShapeDtypeStruct((length, inner), BF16),
        scratch_shapes=[
            pltpu.VMEM((CHUNK + 2 * HALO, channels), F32),
            pltpu.VMEM((2, chunks, CHUNK, channels), BF16),
            pltpu.VMEM((2, chunks, STATE, inner), BF16),
            pltpu.VMEM((2, chunks, CHUNK, inner), BF16),
            pltpu.VMEM((chunks, CHUNK, inner), F32),
            pltpu.VMEM((2, chunks, CHUNK, heads), F32),
            pltpu.VMEM((2, chunks, heads, CHUNK), F32),
            pltpu.VMEM((STATE, inner), F32),
            pltpu.VMEM((8, heads), F32),
            pltpu.VMEM((2, HALO, channels), BF16),
            pltpu.VMEM((2, HALO, channels), BF16),
            pltpu.VMEM((2, n, height + TILE, 128), BF16),
            pltpu.VMEM((2, n, height + TILE, 128), BF16),
            pltpu.VMEM((2, n, height, 128), BF16),
            pltpu.VMEM((2, n, height, 128), BF16),
            pltpu.SemaphoreType.DMA((2,)),
            pltpu.SemaphoreType.DMA((2,)),
            pltpu.SemaphoreType.DMA((4,)),
            pltpu.SemaphoreType.DMA((4,)),
        ],
        compiler_params=pltpu.CompilerParams(
            collective_id=0, has_side_effects=True, vmem_limit_bytes=60 * 1024 * 1024
        ),
    )(
        conv_input,
        conv_input,
        conv_input,
        conv_input,
        conv_input,
        step_raw,
        gate_input,
        filter_taps,
        filter_bias,
        step_bias,
        log_rate,
        jnp.repeat(skip_scale, HEAD_DIM, axis=1),
        norm_gain,
        e2,
        e3,
    )


def solution(mesh):
    return jax.shard_map(
        on_device,
        mesh=mesh,
        in_specs=(P(("groups", "seq"), None),) * 3 + (P(),) * 6,
        out_specs=P(("groups", "seq"), None),
        check_vma=False,
    )
```

time: 203 us -> 99.7 us (0.49)
  the two profiles are of different devices: /device:TPU:0 before, /device:TPU:15 now
where the time goes in v1:
time: 99.7 us; the launch traced here: 99.4 us
  Pallas kernels  89.7 us (90%)
  local copies, waits for them, and re-layouts  7.9 us (8%)
  other arithmetic  1.78 us (2%)
    pallas_call x1, Pallas kernels, on_device(): pl.pallas_call(functools.partial(mixer_kernel, heads, n), grid=(5 * chunk...  89.7 us
    unnamed x2, local copies, waits for them, and re-layouts  6.46 us

profile of v1, /device:TPU:15, one launch (start us, length us, event | category | flops | bytes accessed | tf_op | source)
XLA Modules:
  0.0 99.4 jit_solution(397268284635829455)
XLA Ops:
  0.0 0.8 broadcast_in_dim.3
  0.8 0.7 reshape.3.skip_ref
  1.5 0.8 fusion.1.e2_ref
  2.3 1.7 %copy.10.raw_ref = bf16[1024,32]{1,0:T(8,128)(2,1)} copy(bf16[1024,32]{0,1:T(8,128)(2,1)} %param.11) | data formatting | bytes 131072 | tf_op args[2]
  4.0 0.9 fusion.e3_ref
  4.9 89.7 %shard_map.91 = bf16[1024,2048]{1,0:T(8,128)(2,1)} custom-call(bf16[1024,2304]{1,0:T(8,128)(2,1)} %next_ref.1, bf16[1024,2304]{1,0:T(8,128)(2,1)} %next_ref.1, bf16[1024,2304]{1,0:T(8,128)(2,1)} %next_ref.1, bf16[1024,2304]{1,0:T(8,128)(2,1)} %next_ref.1, bf16[1024,2304]{1,0:T(8,128)(2,1)} %next_ref.1, bf16[1024,32]{1,0:T(8,128)(2,1)} %copy.10.raw_ref, ...), custom_call_target="tpu_custom_call" | custom-call | tf_op jit(solution)/shard_map/pallas_call | solution.py:314
  94.6 4.8 %copy.12 = bf16[1024,2048]{1,0:T(8,128)(2,1)} copy(bf16[1024,2048]{1,0:T(8,128)(2,1)} %shard_map.91) | data formatting | bytes 8388608
  (6 shorter events, 0.0 us)

commit v2 on v1

--- a/solution.py
+++ b/solution.py
@@ -12,6 +12,7 @@
 CHUNK = 128
 HALO = 16
 TILE = 16
+AT = ((1, 5, 9), (1, 5, 9))
 MESH = pl.DeviceIdType.MESH
 LOG2E = 1.4426950408889634
 F32 = jnp.float32
@@ -51,8 +52,6 @@
     lrate_ref,
     skip_ref,
     gain_ref,
-    e2_ref,
-    e3_ref,
     out_ref,
     buf,
     u,
@@ -66,9 +65,15 @@
     edge,
     halo,
     message,
+    other,
+    summary,
     got,
     reply,
     entering,
+    beside,
+    e2_ref,
+    e3_ref,
+    skip,
     edge_send,
     edge_recv,
     send_sem,
@@ -79,6 +84,10 @@
     inner = heads * HEAD_DIM
     channels = cur_ref.shape[1]
     me = lax.axis_index("seq")
+    chips = n // 2
+    chip = me // 2
+    core = lax.rem(me, 2)
+    partner = me + 1 - 2 * core
     height = STATE * (inner // 128) // n
     share = lambda o: (
         slice(o * height % STATE, o * height % STATE + height),
@@ -95,36 +104,54 @@
             device_id_type=MESH,
         )
 
-    def to_all(source, target, number, k):
-        @pl.loop(1, n)
+    def to_partner(source, target, number, k):
+        return pltpu.make_async_remote_copy(
+            src_ref=source.at[k],
+            dst_ref=target.at[k],
+            send_sem=send_sem.at[number, k],
+            recv_sem=recv_sem.at[number, k],
+            device_id={"seq": partner},
+            device_id_type=MESH,
+        )
+
+    def to_chips(source, target, number, k):
+        @pl.loop(1, chips)
         def _(p):
-            peer = lax.rem(me + p, n)
+            peer = lax.rem(chip + p, chips)
             pltpu.make_async_remote_copy(
                 src_ref=source.at[k, peer],
-                dst_ref=target.at[k, me],
-                send_sem=send_sem.at[number],
-                recv_sem=recv_sem.at[number],
-                device_id={"seq": peer},
+                dst_ref=target.at[k, chip],
+                send_sem=send_sem.at[number, k],
+                recv_sem=recv_sem.at[number, k],
+                device_id={"seq": 2 * peer + core},
                 device_id_type=MESH,
             ).start()
 
-    def wait_all(ref, sem, k):
-        part = ref.at[k, pl.ds(0, n - 1)]
-        pltpu.make_async_copy(part, part, sem).wait()
+    def wait_chips(ref, sem, number, k):
+        part = ref.at[k, pl.ds(0, chips - 1)]
+        pltpu.make_async_copy(part, part, sem.at[number, k]).wait()
 
     @pl.when(step == 0)
     def _():
         barrier = pltpu.get_barrier_semaphore()
 
-        @pl.loop(1, n)
+        def greet(peer):
+            pl.semaphore_signal(barrier, inc=1, device_id={"seq": peer}, device_id_type=MESH)
+
+        greet(lax.rem(me + 1, n))
+        greet(lax.rem(me + n - 1, n))
+
+        @pl.loop(1, chips)
         def _(p):
-            pl.semaphore_signal(
-                barrier, inc=1, device_id={"seq": lax.rem(me + p, n)}, device_id_type=MESH
-            )
+            greet(2 * lax.rem(chip + p, chips) + core)
 
         edge[0] = tail_ref[...]
         edge[1] = head_ref[...]
-        pl.semaphore_wait(barrier, n - 1)
+        e2_ref[...] = expander(heads, 2)
+        e3_ref[...] = expander(heads, 3)
+        scales = jnp.concatenate([skip_ref[...]] * 4, axis=0)
+        skip[...] = expand(scales, e3_ref[...])
+        pl.semaphore_wait(barrier, chips + 1)
         to_edge(0).start()
         to_edge(1).start()
 
@@ -159,14 +186,15 @@
                 half = 0.5 * bias_ref[k : k + 1, lanes] + term if half is None else half + term
             u[k, at, :, lanes] = (half + half * jnp.tanh(half)).astype(BF16)
 
-        dt = jax.nn.softplus(raw_ref[...].astype(F32) + sbias_ref[k : k + 1, :])
-        a = dt * (-LOG2E * jnp.exp(lrate_ref[k : k + 1, :]))
-        tri = ((s <= t) if k == 0 else (s >= t)).astype(F32)
-        cum = jnp.dot(tri, a, precision=lax.Precision.HIGHEST, preferred_element_type=F32)
+        dt = jax.nn.softplus(raw_ref[...].astype(F32) + sbias_ref[:, k : k + 1])
+        a = dt * (-LOG2E * jnp.exp(lrate_ref[:, k : k + 1]))
+        tri = ((t <= s) if k == 0 else (t >= s)).astype(F32)
+        across = jnp.dot(a, tri, precision=lax.Precision.HIGHEST, preferred_element_type=F32)
+        rows[k, at] = jnp.log2(dt) - across
+        cum = across.T
+        ahead = rows[k, at].T
         end = cum[CHUNK - 1 : CHUNK] if k == 0 else cum[0:1]
-        ahead = jnp.log2(dt) - cum
         cols[k, at] = cum
-        rows[k, at] = ahead.T
         weight = expand(jnp.exp2(end + ahead), e2_ref[...])
         xs = (u[k, at, :, :inner].astype(F32) * weight).astype(BF16)
         bt = u[k, at, :, inner : inner + STATE].T
@@ -187,21 +215,49 @@
                 where = share(o)
                 message[k, o, 0:height] = state[where].astype(BF16)
                 message[k, o, height:] = tile[:, where[1]].astype(BF16)
-            got[k, me] = message[k, me]
-            to_all(message, got, k, k)
+            to_partner(message, other, 0, k).start()
+
+    def decay_of(tile):
+        return tile[0:1].astype(F32) + tile[1:2].astype(F32)
+
+    def per_chip(k):
+        to_partner(message, other, 0, k).wait()
+        mine_first = core == k
+        which = lax.broadcasted_iota(jnp.int32, (TILE, 128), 0)
+
+        @pl.loop(0, chips)
+        def _(q):
+            o = 2 * q + core
+            mine = message[k, o, 0:height].astype(F32)
+            theirs = other[k, o, 0:height].astype(F32)
+            my_decay = decay_of(message[k, o, height:])
+            their_decay = decay_of(other[k, o, height:])
+            total = jnp.where(mine_first, mine * their_decay + theirs, theirs * my_decay + mine)
+            decay = my_decay * their_decay
+            high = decay.astype(BF16).astype(F32)
+            tile = jnp.where(which == 0, high, jnp.where(which == 1, decay - high, 0.0))
+            summary[k, q, 0:height] = total.astype(BF16)
+            summary[k, q, height:] = tile.astype(BF16)
+
+        got[k, chip] = summary[k, chip]
+        to_chips(summary, got, 1, k)
 
     def scan(k):
-        wait_all(got, recv_sem.at[k], k)
+        wait_chips(got, recv_sem, 1, k)
 
         def one(j, held):
-            j = j if k == 0 else n - 1 - j
+            j = j if k == 0 else chips - 1 - j
             reply[k, j] = held.astype(BF16)
-            tile = got[k, j, height:].astype(F32)
-            return held * (tile[0:1] + tile[1:2]) + got[k, j, 0:height].astype(F32)
-
-        lax.fori_loop(0, n, one, jnp.zeros((height, 128), F32))
-        entering[k, me] = reply[k, me]
-        to_all(reply, entering, 2 + k, k)
+            decay = decay_of(got[k, j, height:])
+            return held * decay + got[k, j, 0:height].astype(F32)
+
+        lax.fori_loop(0, chips, one, jnp.zeros((height, 128), F32))
+        entering[k, chip] = reply[k, chip]
+        to_chips(reply, entering, 2, k)
+
+    def back(k):
+        wait_chips(entering, recv_sem, 2, k)
+        to_partner(entering, beside, 3, k).start()
 
     def diagonal(k, at):
         b = u[k, at, :, inner : inner + STATE]
@@ -220,14 +276,20 @@
                 [jnp.where(s < HEAD_DIM, x, zero), jnp.where(s >= HEAD_DIM, x, zero)], axis=0
             )
             y = jnp.dot(jnp.concatenate(weights, axis=1), both, preferred_element_type=F32)
-            local[k, at, :, lanes] = (y + x.astype(F32) * skip_ref[k : k + 1, lanes]).astype(BF16)
+            local[k, at, :, lanes] = (y + x.astype(F32) * skip[k : k + 1, lanes]).astype(BF16)
 
     def finish(k, at, first):
         @pl.when(first)
         def _():
-            wait_all(entering, recv_sem.at[2 + k], k)
+            to_partner(entering, beside, 3, k).wait()
+            mine_first = core == k
             for o in range(n):
-                state[share(o)] = entering[k, o].astype(F32)
+                own = core == o % 2
+                enter = jnp.where(
+                    own, entering[k, o // 2].astype(F32), beside[k, o // 2].astype(F32)
+                )
+                after = enter * decay_of(other[k, o, height:]) + other[k, o, 0:height].astype(F32)
+                state[share(o)] = jnp.where(mine_first, enter, after)
 
         cum = cols[k, at]
         end = cum[CHUNK - 1 : CHUNK] if k == 0 else cum[0:1]
@@ -251,13 +313,9 @@
     def _():
         prepare(1, step - chunks, step == chunks, step == 2 * chunks - 1)
 
-    @pl.when(step == 2 * chunks)
-    def _():
-        scan(0)
-
-    @pl.when(step == 3 * chunks - 2)
-    def _():
-        scan(1)
+    for k in range(2):
+        for number, stage in enumerate((per_chip, scan, back)):
+            pl.when(step == (1 + k) * chunks + AT[k][number])(functools.partial(stage, k))
 
     @pl.when((step >= 2 * chunks) & (step < 3 * chunks))
     def _():
@@ -278,8 +336,8 @@
     @pl.when(step == 5 * chunks - 1)
     def _():
         for k in range(2):
-            wait_all(message, send_sem.at[k], k)
-            wait_all(reply, send_sem.at[2 + k], k)
+            wait_chips(summary, send_sem, 1, k)
+            wait_chips(reply, send_sem, 2, k)
 
 
 def on_device(
@@ -299,8 +357,6 @@
     chunks = length // CHUNK
     n = lax.axis_size("seq")
     height = STATE * (inner // 128) // n
-    e2 = expander(heads, 2)
-    e3 = expander(heads, 3)
     per = CHUNK // HALO
     last = chunks * per - 1
     whole = lambda *shape: pl.BlockSpec(shape, lambda *_: (0,) * len(shape))
@@ -320,16 +376,14 @@
             pl.BlockSpec((HALO, channels), lambda i: (jnp.maximum(taken(i) * per - 1, 0), 0)),
             pl.BlockSpec((CHUNK, channels), lambda i: (taken(i), 0)),
             pl.BlockSpec((HALO, channels), lambda i: (jnp.minimum(taken(i) * per + per, last), 0)),
-            pl.BlockSpec((CHUNK, heads), lambda i: (taken(i), 0)),
+            pl.BlockSpec((heads, CHUNK), lambda i: (0, taken(i))),
             pl.BlockSpec((CHUNK, inner), lambda i: (given(i), 0)),
             whole(*filter_taps.shape),
             whole(*filter_bias.shape),
-            whole(2, heads),
+            whole(heads, 2),
+            whole(heads, 2),
             whole(2, heads),
             whole(2, inner),
-            whole(2, inner),
-            whole(*e2.shape),
-            whole(*e3.shape),
         ],
         out_specs=pl.BlockSpec(
             (CHUNK, inner), lambda i: (jnp.minimum(5 * chunks - 1 - i, chunks - 1), 0)
@@ -349,12 +403,18 @@
             pltpu.VMEM((2, HALO, channels), BF16),
             pltpu.VMEM((2, n, height + TILE, 128), BF16),
             pltpu.VMEM((2, n, height + TILE, 128), BF16),
-            pltpu.VMEM((2, n, height, 128), BF16),
-            pltpu.VMEM((2, n, height, 128), BF16),
+            pltpu.VMEM((2, n // 2, height + TILE, 128), BF16),
+            pltpu.VMEM((2, n // 2, height + TILE, 128), BF16),
+            pltpu.VMEM((2, n // 2, height, 128), BF16),
+            pltpu.VMEM((2, n // 2, height, 128), BF16),
+            pltpu.VMEM((2, n // 2, height, 128), BF16),
+            pltpu.VMEM((2 * heads, inner), BF16),
+            pltpu.VMEM((3 * heads, inner), BF16),
+            pltpu.VMEM((8, inner), F32),
             pltpu.SemaphoreType.DMA((2,)),
             pltpu.SemaphoreType.DMA((2,)),
-            pltpu.SemaphoreType.DMA((4,)),
-            pltpu.SemaphoreType.DMA((4,)),
+            pltpu.SemaphoreType.DMA((4, 2)),
+            pltpu.SemaphoreType.DMA((4, 2)),
         ],
         compiler_params=pltpu.CompilerParams(
             collective_id=0, has_side_effects=True, vmem_limit_bytes=60 * 1024 * 1024
@@ -365,16 +425,14 @@
         conv_input,
         conv_input,
         conv_input,
-        step_raw,
+        step_raw.T,
         gate_input,
         filter_taps,
         filter_bias,
-        step_bias,
-        log_rate,
-        jnp.repeat(skip_scale, HEAD_DIM, axis=1),
+        step_bias.T,
+        log_rate.T,
+        skip_scale,
         norm_gain,
-        e2,
-        e3,
     )
 
 

time: 99.7 us -> 87.9 us (0.88)
  the two profiles are of different devices: /device:TPU:15 before, /device:TPU:0 now
where the time goes in v2:
time: 87.9 us; the launch traced here: 87.7 us
  Pallas kernels  80.2 us (91%)
  local copies, waits for them, and re-layouts  7.5 us (9%)
    pallas_call x1, Pallas kernels, on_device(): pl.pallas_call(functools.partial(mixer_kernel, heads, n), grid=(5 * chunk...  80.2 us
    unnamed x3, local copies, waits for them, and re-layouts  7.5 us

profile of v2, /device:TPU:0, one launch (start us, length us, event | category | flops | bytes accessed | tf_op | source)
XLA Modules:
  0.0 87.7 jit_solution(13818538466605523287)
XLA Ops:
  0.0 1.4 %copy.10 = f32[2,32]{0,1:T(8,128)} copy(f32[2,32]{1,0:T(2,128)} %param.14) | data formatting | bytes 512 | tf_op args[5]
  1.4 1.4 %copy.11 = f32[2,32]{0,1:T(8,128)} copy(f32[2,32]{1,0:T(2,128)} %param.15) | data formatting | bytes 512 | tf_op args[6]
  2.7 80.2 %shard_map.91 = bf16[1024,2048]{1,0:T(8,128)(2,1)} custom-call(bf16[1024,2304]{1,0:T(8,128)(2,1)} %next_ref.1, bf16[1024,2304]{1,0:T(8,128)(2,1)} %next_ref.1, bf16[1024,2304]{1,0:T(8,128)(2,1)} %next_ref.1, bf16[1024,2304]{1,0:T(8,128)(2,1)} %next_ref.1, bf16[1024,2304]{1,0:T(8,128)(2,1)} %next_ref.1, bf16[32,1024]{1,0:T(8,128)(2,1)} %bitcast.3, ...), custom_call_target="tpu_custom_call" | custom-call | tf_op jit(solution)/shard_map/pallas_call | solution.py:370
  82.9 4.8 %copy.13 = bf16[1024,2048]{1,0:T(8,128)(2,1)} copy(bf16[1024,2048]{1,0:T(8,128)(2,1)} %shard_map.91) | data formatting | bytes 8388608

commit v3 on v2

--- a/solution.py
+++ b/solution.py
@@ -12,7 +12,7 @@
 CHUNK = 128
 HALO = 16
 TILE = 16
-AT = ((1, 5, 9), (1, 5, 9))
+AT = ((2, 6, 11), (2, 6, 12))
 MESH = pl.DeviceIdType.MESH
 LOG2E = 1.4426950408889634
 F32 = jnp.float32

time: 87.9 us -> 88.3 us (level)
  no operation moved by 1% of the time
where the time goes in v3:
time: 88.3 us; the launch traced here: 88.1 us
  Pallas kernels  80.6 us (91%)
  local copies, waits for them, and re-layouts  7.5 us (8%)
    pallas_call x1, Pallas kernels, on_device(): pl.pallas_call(functools.partial(mixer_kernel, heads, n), grid=(5 * chunk...  80.6 us
    unnamed x3, local copies, waits for them, and re-layouts  7.5 us

profile of v3, /device:TPU:0, one launch (start us, length us, event | category | flops | bytes accessed | tf_op | source)
XLA Modules:
  0.0 88.1 jit_solution(4562044660069574143)
XLA Ops:
  0.0 1.4 %copy.10 = f32[2,32]{0,1:T(8,128)} copy(f32[2,32]{1,0:T(2,128)} %param.14) | data formatting | bytes 512 | tf_op args[5]
  1.4 1.4 %copy.11 = f32[2,32]{0,1:T(8,128)} copy(f32[2,32]{1,0:T(2,128)} %param.15) | data formatting | bytes 512 | tf_op args[6]
  2.7 80.6 %shard_map.91 = bf16[1024,2048]{1,0:T(8,128)(2,1)} custom-call(bf16[1024,2304]{1,0:T(8,128)(2,1)} %next_ref.1, bf16[1024,2304]{1,0:T(8,128)(2,1)} %next_ref.1, bf16[1024,2304]{1,0:T(8,128)(2,1)} %next_ref.1, bf16[1024,2304]{1,0:T(8,128)(2,1)} %next_ref.1, bf16[1024,2304]{1,0:T(8,128)(2,1)} %next_ref.1, bf16[32,1024]{1,0:T(8,128)(2,1)} %bitcast.3, ...), custom_call_target="tpu_custom_call" | custom-call | tf_op jit(solution)/shard_map/pallas_call | solution.py:370
  83.3 4.8 %copy.13 = bf16[1024,2048]{1,0:T(8,128)(2,1)} copy(bf16[1024,2048]{1,0:T(8,128)(2,1)} %shard_map.91) | data formatting | bytes 8388608
